TPU v7x, 32 devices: a whole 2x2x4 slice. The times are simulated.
32 devices in a mesh: row: 4 (over y, core), col: 8 (over z, x).
Axes of the slice: x: 2, y: 2, z: 4, core: 2. Of those that a mesh axis runs over, the one named last changes fastest.
Arguments:
- transition: bfloat16 [32768, 32768], P('row', 'col'), may hold values from 1.5258789e-06 to 0.0024414062, as said below
- emission: bfloat16 [96, 32768], P(None, 'col'), may hold values from 0.0099487305 to 1
- token_ids: int32 [2, 192], replicated, may hold values from 0 to 95
- forward: bfloat16 [2, 192, 32768], P(None, 'col', 'row'), may hold values from 3.0517578e-06 to 0.0008239746, as said below
- backward_last: float32 [192, 32768], P('row', 'col'), may hold values from 0.1 to 10
Outputs:
- backward: float32 [2, 192, 32768], P(None, 'col', 'row')
- counts: float32 [32768, 1024], P('row', 'col')
Inputs may be any that keep to these rules, and one draw needn't show every extreme that they name: Positive transition weights. Positive forward weights.
All inputs are finite; a program needn't handle non-finite values.
Results may differ from a plain program's by a relative error of at most 0.00048.
Values may be sent and summed in bfloat16 or wider, within the bound.
A program may use at most 192 MiB of HBM per device.

v0:
```python
import jax
import jax.numpy as jnp
from jax import lax
from jax.sharding import PartitionSpec as P

H = 32768
N = 192
DW = 128


def spread(value, axis, source):
    kept = jnp.where(lax.axis_index(axis) == source, value, 0).astype(value.dtype)
    return lax.psum(kept, axis)


def on_device(transition, emission, token_ids, forward, backward_last):
    row_count = lax.axis_size("row")
    col_count = lax.axis_size("col")
    col_index = lax.axis_index("col")
    ratio = col_count // row_count
    local_seqs = forward.shape[1]
    block_src = transition.shape[0]
    block_dst = transition.shape[1]
    seq_total = local_seqs * col_count
    forward_all = lax.all_gather(forward, "col", axis=1, tiled=True)
    backward_next = lax.all_gather(backward_last, "row", axis=0, tiled=True)
    columns = lax.broadcasted_iota(jnp.int32, (seq_total, emission.shape[0]), 1)
    window = transition[:, :DW]
    totals = jnp.zeros((block_src, DW), jnp.float32)
    outputs = [None, None]
    for step in (1, 0):
        onehot = (token_ids[step][:, None] == columns).astype(jnp.bfloat16)
        emitted = jnp.dot(onehot, emission, preferred_element_type=jnp.float32)
        weighted_back = (emitted * backward_next).astype(jnp.bfloat16)
        partial_value = lax.dot_general(
            weighted_back, transition, (((1,), (1,)), ((), ())), preferred_element_type=jnp.float32
        )
        alpha_all = forward_all[step].astype(jnp.float32)
        summed = lax.psum(partial_value, "col")
        mine = lax.dynamic_slice_in_dim(summed, col_index * local_seqs, local_seqs, 0)
        alpha_mine = forward[step].astype(jnp.float32)
        local_norm = lax.psum(jnp.sum(alpha_mine * mine, axis=1), "row")
        normal_all = lax.all_gather(local_norm, "col", axis=0, tiled=True)
        normal_mine = lax.dynamic_slice_in_dim(normal_all, col_index * local_seqs, local_seqs, 0)
        outputs[step] = mine / normal_mine[:, None]
        scaled = (alpha_all / normal_all[:, None]).astype(jnp.bfloat16)
        totals = totals + lax.dot_general(
            scaled,
            weighted_back[:, :DW],
            (((0,), (0,)), ((), ())),
            preferred_element_type=jnp.float32,
        )
        if step == 1:
            whole = summed / normal_all[:, None]
            piece = lax.dynamic_slice_in_dim(whole, col_index % ratio * block_dst, block_dst, 1)
            backward_next = spread(piece, "row", col_index // ratio)
    counts = window.astype(jnp.float32) * totals * (H * H / N)
    return (jnp.stack(outputs), counts)


def solution(mesh):
    in_specs = (P("row", "col"), P(None, "col"), P(), P(None, "col", "row"), P("row", "col"))
    out_specs = (P(None, "col", "row"), P("row", "col"))
    return jax.shard_map(
        on_device, mesh=mesh, in_specs=in_specs, out_specs=out_specs, check_vma=False
    )
```

profile of v0, /device:TPU:0, one launch (start us, length us, event | category | flops | bytes accessed | tf_op | source)
XLA Modules:
  0.0 741.6 jit_solution(9007567216397277755)
XLA Ops:
  7.2 0.7 all-gather.3.cloned.1.call-update
  8.0 0.8 fusion.17
  8.7 32.1 %all-gather.3.cloned.1.call-done = f32[192,4096]{1,0:T(8,128)} async-done(((f32[48,4096]{1,0:T(8,128)}), f32[192,4096]{1,0:T(8,128)}) %all-gather.3.cloned.1.call-update) | async-done | bytes 3145744 | tf_op jit(solution)/shard_map/all_gather | solution.py:26
  40.8 2.5 fusion.5
  43.3 31.1 %fusion.18 = f32[192,8192]{1,0:T(8,128)} fusion(bf16[192,4096]{1,0:T(8,128)(2,1)S(1)} %fusion.5, bf16[8192,4096]{1,0:T(8,128)(2,1)} %param.5), kind=kOutput, calls=%fused_computation.31 | convolution fusion | flops 12884901888 | bytes 74973184 | tf_op jit(solution)/shard_map/dot_general | solution.py:35
  75.1 0.6 dynamic-slice
  76.4 209.8 %all-reduce.6.cloned.1.call-done = f32[192,8192]{1,0:T(8,128)} async-done(((f32[192,8192]{1,0:T(8,128)}), f32[192,8192]{1,0:T(8,128)}) %all-reduce.6.cloned.1.call-update) | async-done | bytes 6291472 | tf_op jit(solution)/shard_map/psum | solution.py:39
  286.2 1.3 fusion.12
  287.5 6.9 psum.36
  294.7 19.4 %all-reduce = f32[192]{0:T(256)S(1)} all-reduce(f32[192]{0:T(256)S(1)} %dynamic-update-slice), channel_id=1, replica_groups=mesh['row'=4,'col'=8] {'col'}, use_global_device_ids=true, to_apply=%add | all-reduce | flops 192 | bytes 1536
  314.1 4.0 fusion.7
  318.7 64.3 %all-reduce.8.cloned.1.call-done = f32[192,4096]{1,0:T(8,128)} async-done(((f32[192,4096]{1,0:T(8,128)}), f32[192,4096]{1,0:T(8,128)}) %all-reduce.8.cloned.1.call-update) | async-done | bytes 3145744 | tf_op jit(solution)/shard_map/psum | solution.py:13
  383.0 3.7 fusion.4
  386.7 30.8 %fusion.19 = f32[192,8192]{1,0:T(8,128)} fusion(bf16[192,4096]{1,0:T(8,128)(2,1)} %fusion.4, bf16[8192,4096]{1,0:T(8,128)(2,1)} %param.5), kind=kOutput, calls=%fused_computation.32 | convolution fusion | flops 12884901888 | bytes 74973184 | tf_op jit(solution)/shard_map/dot_general | solution.py:35
  417.6 66.8 %all-gather.5.cloned.1.call-done = bf16[2,192,8192]{2,1,0:T(8,128)(2,1)} async-done(((bf16[2,24,8192]{2,1,0:T(8,128)(2,1)}), bf16[2,192,8192]{2,1,0:T(8,128)(2,1)}) %all-gather.5.cloned.1.call-update) | async-done | bytes 6291472 | tf_op jit(solution)/shard_map/all_gather | solution.py:25
  484.4 5.4 fusion.9
  489.9 1.3 divide_bitcast_fusion
  491.1 207.2 %all-reduce.10.cloned.1.call-done = f32[192,8192]{1,0:T(8,128)} async-done(((f32[192,8192]{1,0:T(8,128)}), f32[192,8192]{1,0:T(8,128)}) %all-reduce.10.cloned.1.call-update) | async-done | bytes 6291472 | tf_op jit(solution)/shard_map/psum | solution.py:39
  698.3 1.3 fusion.11
  699.6 6.9 psum.39
  706.7 19.4 %all-reduce.1 = f32[192]{0:T(256)S(1)} all-reduce(f32[192]{0:T(256)S(1)} %dynamic-update-slice.1), channel_id=1, replica_groups=mesh['row'=4,'col'=8] {'col'}, use_global_device_ids=true, to_apply=%add.1 | all-reduce | flops 192 | bytes 1536
  726.2 1.4 divide_bitcast_fusion.1
  727.6 1.2 pad_maximum_fusion
  728.9 6.2 fusion.1
  (25 shorter events, 2.0 us)
Async XLA Ops:
  7.2 33.7 %copy-start = (bf16[96,4096]{1,0:T(8,128)(2,1)S(1)}, bf16[96,4096]{1,0:T(8,128)(2,1)}, u32[]{:S(2)}) copy-start(bf16[96,4096]{1,0:T(8,128)(2,1)} %param.6) | copy-start | bytes 2359300
  7.2 33.7 %all-gather.3.cloned.1.call-start = ((), (), s32[]{:S(2)}) async-start(), calls=%async_computation | async-start | bytes 3932160 | tf_op jit(solution)/shard_map/all_gather | solution.py:26
  7.9 278.3 %all-reduce.6.cloned.1.call-start = ((), (), s32[]{:S(2)}) async-start(), calls=%async_computation.1 | async-start | bytes 12582912 | tf_op jit(solution)/shard_map/psum | solution.py:39
  74.5 0.7 copy-start.3
  74.5 211.8 %copy-start.1 = (bf16[2,24,8192]{2,1,0:T(8,128)(2,1)S(1)}, bf16[2,24,8192]{2,1,0:T(8,128)(2,1)}, u32[]{:S(2)}) copy-start(bf16[2,24,8192]{2,1,0:T(8,128)(2,1)} %param.8) | copy-start | bytes 2359300
  74.5 308.5 %all-reduce.8.cloned.1.call-start = ((), (), s32[]{:S(2)}) async-start(), calls=%async_computation.2 | async-start | bytes 6291456 | tf_op jit(solution)/shard_map/psum | solution.py:13
  318.1 166.4 %all-gather.5.cloned.1.call-start = ((), (), s32[]{:S(2)}) async-start(), calls=%async_computation.4 | async-start | bytes 7077888 | tf_op jit(solution)/shard_map/all_gather | solution.py:25
  318.7 379.7 %all-reduce.10.cloned.1.call-start = ((), (), s32[]{:S(2)}) async-start(), calls=%async_computation.3 | async-start | bytes 12582912 | tf_op jit(solution)/shard_map/psum | solution.py:39
  417.6 280.7 %copy-start.2 = (bf16[2,24,8192]{2,1,0:T(8,128)(2,1)S(1)}, bf16[2,24,8192]{2,1,0:T(8,128)(2,1)}, u32[]{:S(2)}) copy-start(bf16[2,24,8192]{2,1,0:T(8,128)(2,1)} %param.8) | copy-start | bytes 2359300
  726.1 2.7 copy-start.4
Sparse Core Ops, SparseCore 0:
  9.6 31.2 all-gather.2
  74.6 211.5 all-reduce.5
  318.2 64.7 all-reduce.7
  385.3 99.1 all-gather.4
  488.5 209.7 all-reduce.9
where the time goes:
time: 742 us
  waiting for transfers between devices  582 us (78%)
  matrix products  79.7 us (11%)
  blocking collectives  52.5 us (7%)
  between operations  14.5 us (2%)
  other arithmetic  10.5 us (1%)
    psum x2, waiting for transfers between devices, on_device(): summed = lax.psum(partial_value, 'col')  417 us
    all_gather x1, waiting for transfers between devices, on_device(): forward_all = lax.all_gather(forward, 'col', axis=1, tiled=True)  66.8 us
    psum x1, waiting for transfers between devices, spread(): return lax.psum(kept, axis)  64.3 us
    dot_general x2, matrix products, on_device(): lax.dot_general(weighted_back, transition, (((1,), (1,)), ((), ())), pref...  61.9 us
    unnamed x2, blocking collectives  38.8 us
    all_gather x1, waiting for transfers between devices, on_device(): backward_next = lax.all_gather(backward_last, 'row', axis=0, tiled=True)  32.1 us
  transfers between devices with their start and end apart: 5, of which 5 were waited for; matrix products, arithmetic and copies ran while one was open for 6% of the time, Pallas kernels for 0%

commit v1 on v0

--- a/solution.py
+++ b/solution.py
@@ -22,7 +22,12 @@
     block_src = transition.shape[0]
     block_dst = transition.shape[1]
     seq_total = local_seqs * col_count
-    forward_all = lax.all_gather(forward, "col", axis=1, tiled=True)
+    ring = [forward]
+    for hop in range(7):
+        ring.append(lax.ppermute(ring[-1], "col", [(dev, (dev + 1) % 8) for dev in range(8)]))
+    forward_all = jnp.roll(
+        jnp.concatenate(ring[::-1], axis=1), (lax.axis_index("col") + 1) * ring[0].shape[1], axis=1
+    )
     backward_next = lax.all_gather(backward_last, "row", axis=0, tiled=True)
     columns = lax.broadcasted_iota(jnp.int32, (seq_total, emission.shape[0]), 1)
     window = transition[:, :DW]

time: 742 us -> 766 us (1.032)
  local copies, waits for them, and re-layouts: 2.54 us -> 29.1 us
  waiting for transfers between devices: 582 us -> 573 us
    ppermute x0 -> x7, waiting for transfers between devices: none -> 116 us  [on_device(): lax.ppermute(ring[-1], 'col', [(dev, (dev + 1) % 8) for dev in range(8)])]
    all_gather x1 -> x0, waiting for transfers between devices: 66.8 us -> none  [on_device(): forward_all = lax.all_gather(forward, 'col', axis=1, tiled=True)]
    all_gather x1, waiting for transfers between devices: 32.1 us -> 0.01 us  [on_device(): backward_next = lax.all_gather(backward_last, 'row', axis=0, tiled=True)]
    unnamed x15 -> x36, local copies, waits for them, and re-layouts: 1.62 us -> 27.2 us
    psum x2, waiting for transfers between devices: 417 us -> 396 us  [on_device(): summed = lax.psum(partial_value, 'col')]
  transfers between devices with their start and end apart: 5 -> 11, of which waited for: 5 -> 9; matrix products, arithmetic and copies ran while one was open for 6% -> 9% of each run, Pallas kernels for 0% -> 0%
where the time goes in v1:
time: 766 us; the launch traced here: 765 us
  waiting for transfers between devices  573 us (75%)
  matrix products  81.9 us (11%)
  blocking collectives  52.5 us (7%)
  local copies, waits for them, and re-layouts  29.1 us (4%)
  between operations  14.5 us (2%)
  other arithmetic  10.4 us (1%)
    psum x2, waiting for transfers between devices, on_device(): summed = lax.psum(partial_value, 'col')  396 us
    ppermute x7, waiting for transfers between devices, on_device(): lax.ppermute(ring[-1], 'col', [(dev, (dev + 1) % 8) for dev in range(8)])  116 us
    dot_general x2, matrix products, on_device(): lax.dot_general(weighted_back, transition, (((1,), (1,)), ((), ())), pref...  61.3 us
    psum x1, waiting for transfers between devices, spread(): return lax.psum(kept, axis)  60.5 us
    unnamed x2, blocking collectives  38.8 us
    unnamed x36, local copies, waits for them, and re-layouts  27.2 us
  transfers between devices with their start and end apart: 11, of which 9 were waited for; matrix products, arithmetic and copies ran while one was open for 9% of the time, Pallas kernels for 0%

profile of v1, /device:TPU:0, one launch (start us, length us, event | category | flops | bytes accessed | tf_op | source)
XLA Modules:
  0.0 764.5 jit_solution(13061276671822395665)
XLA Ops:
  7.2 3.0 collective-permute-start
  10.3 20.7 %collective-permute-done = bf16[2,24,8192]{2,1,0:T(8,128)(2,1)S(1)} collective-permute-done((bf16[2,24,8192]{2,1,0:T(8,128)(2,1)}, bf16[2,24,8192]{2,1,0:T(8,128)(2,1)S(1)}, u32[]{:S(2)}, u32[]{:S(2)}) %collective-permute-start) | collective-permute-done | bytes 786464 | tf_op jit(solution)/shard_map/ppermute | solution.py:27
  31.0 21.4 %collective-permute-done.1 = bf16[2,24,8192]{2,1,0:T(8,128)(2,1)S(1)} collective-permute-done((bf16[2,24,8192]{2,1,0:T(8,128)(2,1)S(1)}, bf16[2,24,8192]{2,1,0:T(8,128)(2,1)S(1)}, u32[]{:S(2)}, u32[]{:S(2)}) %collective-permute-start.1) | collective-permute-done | bytes 786464 | tf_op jit(solution)/shard_map/ppermute | solution.py:27
  52.4 20.5 %collective-permute-done.2 = bf16[2,24,8192]{2,1,0:T(8,128)(2,1)S(1)} collective-permute-done((bf16[2,24,8192]{2,1,0:T(8,128)(2,1)S(1)}, bf16[2,24,8192]{2,1,0:T(8,128)(2,1)S(1)}, u32[]{:S(2)}, u32[]{:S(2)}) %collective-permute-start.2) | collective-permute-done | bytes 786464 | tf_op jit(solution)/shard_map/ppermute | solution.py:27
  73.8 19.6 %collective-permute-done.3 = bf16[2,24,8192]{2,1,0:T(8,128)(2,1)S(1)} collective-permute-done((bf16[2,24,8192]{2,1,0:T(8,128)(2,1)S(1)}, bf16[2,24,8192]{2,1,0:T(8,128)(2,1)S(1)}, u32[]{:S(2)}, u32[]{:S(2)}) %collective-permute-start.3) | collective-permute-done | bytes 786464 | tf_op jit(solution)/shard_map/ppermute | solution.py:27
  94.3 18.7 %collective-permute-done.4 = bf16[2,24,8192]{2,1,0:T(8,128)(2,1)S(1)} collective-permute-done((bf16[2,24,8192]{2,1,0:T(8,128)(2,1)S(1)}, bf16[2,24,8192]{2,1,0:T(8,128)(2,1)S(1)}, u32[]{:S(2)}, u32[]{:S(2)}) %collective-permute-start.4) | collective-permute-done | bytes 786464 | tf_op jit(solution)/shard_map/ppermute | solution.py:27
  115.7 15.1 %collective-permute-done.5 = bf16[2,24,8192]{2,1,0:T(8,128)(2,1)} collective-permute-done((bf16[2,24,8192]{2,1,0:T(8,128)(2,1)S(1)}, bf16[2,24,8192]{2,1,0:T(8,128)(2,1)}, u32[]{:S(2)}, u32[]{:S(2)}) %collective-permute-start.5) | collective-permute-done | bytes 786464 | tf_op jit(solution)/shard_map/ppermute | solution.py:27
  130.8 3.6 fusion.5
  134.5 30.7 %fusion.20 = f32[192,8192]{1,0:T(8,128)} fusion(bf16[192,4096]{1,0:T(8,128)(2,1)} %fusion.5, bf16[8192,4096]{1,0:T(8,128)(2,1)} %param.5), kind=kOutput, calls=%fused_computation.49 | convolution fusion | flops 12884901888 | bytes 74973184 | tf_op jit(solution)/shard_map/dot_general | solution.py:40
  165.2 2.2 constant_dynamic-update-slice_fusion.15
  177.6 2.1 constant_dynamic-update-slice_fusion.7
  179.7 197.4 %all-reduce.6.cloned.1.call-done = f32[192,8192]{1,0:T(8,128)} async-done(((f32[192,8192]{1,0:T(8,128)}), f32[192,8192]{1,0:T(8,128)}) %all-reduce.6.cloned.1.call-update) | async-done | bytes 6291472 | tf_op jit(solution)/shard_map/psum | solution.py:44
  378.4 6.9 psum.36
  385.5 19.4 %all-reduce = f32[192]{0:T(256)S(1)} all-reduce(f32[192]{0:T(256)S(1)} %dynamic-update-slice), channel_id=1, replica_groups=mesh['row'=4,'col'=8] {'col'}, use_global_device_ids=true, to_apply=%add | all-reduce | flops 192 | bytes 1536
  404.9 4.0 fusion.7
  413.3 60.5 %all-reduce.8.cloned.1.call-done = f32[192,4096]{1,0:T(8,128)} async-done(((f32[192,4096]{1,0:T(8,128)}), f32[192,4096]{1,0:T(8,128)}) %all-reduce.8.cloned.1.call-update) | async-done | bytes 3145744 | tf_op jit(solution)/shard_map/psum | solution.py:13
  473.8 3.7 fusion.4
  477.5 30.7 %fusion.21 = f32[192,8192]{1,0:T(8,128)} fusion(bf16[192,4096]{1,0:T(8,128)(2,1)} %fusion.4, bf16[8192,4096]{1,0:T(8,128)(2,1)} %param.5), kind=kOutput, calls=%fused_computation.50 | convolution fusion | flops 12884901888 | bytes 74973184 | tf_op jit(solution)/shard_map/dot_general | solution.py:40
  508.2 2.2 constant_dynamic-update-slice_fusion.4
  514.3 5.4 fusion.9
  521.0 198.8 %all-reduce.10.cloned.1.call-done = f32[192,8192]{1,0:T(8,128)} async-done(((f32[192,8192]{1,0:T(8,128)}), f32[192,8192]{1,0:T(8,128)}) %all-reduce.10.cloned.1.call-update) | async-done | bytes 6291472 | tf_op jit(solution)/shard_map/psum | solution.py:44
  721.1 6.9 psum.39
  728.2 19.4 %all-reduce.1 = f32[192]{0:T(256)S(1)} all-reduce(f32[192]{0:T(256)S(1)} %dynamic-update-slice.1), channel_id=1, replica_groups=mesh['row'=4,'col'=8] {'col'}, use_global_device_ids=true, to_apply=%add.1 | all-reduce | flops 192 | bytes 1536
  747.7 7.8 %fusion.1 = f32[8192,128]{1,0:T(8,128)} fusion(f32[8192,128]{1,0:T(8,128)} %fusion.9, bf16[2,384,8192]{2,1,0:T(8,128)(2,1)} %constant_dynamic-update-slice_fusion, s32[]{:T(128)S(6)} %select_n.47, f32[192]{0:T(256)S(1)} %all-reduce.1, bf16[8192,4096]{1,0:T(8,128)(2,1)} %param.5, bf16[192,4096]{1,0:T(8,128)(2,1)} %fusion.4), kind=kOutput, calls=%fused_computation.2 | convolution fusion | flops 411566080 | bytes 13681412 | tf_op jit(solution)/shard_map/dot_general | solution.py:52
  (58 shorter events, 29.4 us)
Async XLA Ops:
  7.2 123.7 %copy-start = (bf16[96,4096]{1,0:T(8,128)(2,1)S(1)}, bf16[96,4096]{1,0:T(8,128)(2,1)}, u32[]{:S(2)}) copy-start(bf16[96,4096]{1,0:T(8,128)(2,1)} %param.6) | copy-start | bytes 2359300
  7.2 123.6 %all-gather.2.cloned.1.call-start = ((), (), s32[]{:S(2)}) async-start(), calls=%async_computation | async-start | bytes 3932160 | tf_op jit(solution)/shard_map/all_gather | solution.py:31
  7.2 23.8 %collective-permute-start = (bf16[2,24,8192]{2,1,0:T(8,128)(2,1)}, bf16[2,24,8192]{2,1,0:T(8,128)(2,1)S(1)}, u32[]{:S(2)}, u32[]{:S(2)}) collective-permute-start(bf16[2,24,8192]{2,1,0:T(8,128)(2,1)} %param.8), channel_id=1, source_target_pairs={{0,1},{1,2},{2,3},{3,4},{4,5},{5,6},{6,7},{7,0},{8,9},{9,10},{10,1... | collective-permute-start | bytes 2359304 | tf_op jit(solution)/shard_map/ppermute | solution.py:27
  10.2 366.8 %all-reduce.6.cloned.1.call-start = ((), (), s32[]{:S(2)}) async-start(), calls=%async_computation.1 | async-start | bytes 12582912 | tf_op jit(solution)/shard_map/psum | solution.py:44
  31.0 21.4 %collective-permute-start.1 = (bf16[2,24,8192]{2,1,0:T(8,128)(2,1)S(1)}, bf16[2,24,8192]{2,1,0:T(8,128)(2,1)S(1)}, u32[]{:S(2)}, u32[]{:S(2)}) collective-permute-start(bf16[2,24,8192]{2,1,0:T(8,128)(2,1)S(1)} %collective-permute-done), channel_id=1, source_target_pairs={{0,1},{1,2},{2,3},{3,4},{4,5},{5,6},{6,7},{7,0},{8,9},{9,10},{10,1... | collective-permute-start | bytes 2359304 | tf_op jit(solution)/shard_map/ppermute | solution.py:27
  52.4 20.5 %collective-permute-start.2 = (bf16[2,24,8192]{2,1,0:T(8,128)(2,1)S(1)}, bf16[2,24,8192]{2,1,0:T(8,128)(2,1)S(1)}, u32[]{:S(2)}, u32[]{:S(2)}) collective-permute-start(bf16[2,24,8192]{2,1,0:T(8,128)(2,1)S(1)} %collective-permute-done.1), channel_id=1, source_target_pairs={{0,1},{1,2},{2,3},{3,4},{4,5},{5,6},{6,7},{7,0},{8,9},{9,10},{10,1... | collective-permute-start | bytes 2359304 | tf_op jit(solution)/shard_map/ppermute | solution.py:27
  72.9 0.9 copy-start.3
  73.8 19.6 %collective-permute-start.3 = (bf16[2,24,8192]{2,1,0:T(8,128)(2,1)S(1)}, bf16[2,24,8192]{2,1,0:T(8,128)(2,1)S(1)}, u32[]{:S(2)}, u32[]{:S(2)}) collective-permute-start(bf16[2,24,8192]{2,1,0:T(8,128)(2,1)S(1)} %collective-permute-done.2), channel_id=1, source_target_pairs={{0,1},{1,2},{2,3},{3,4},{4,5},{5,6},{6,7},{7,0},{8,9},{9,10},{10,1... | collective-permute-start | bytes 2359304 | tf_op jit(solution)/shard_map/ppermute | solution.py:27
  93.4 0.9 copy-start.6
  94.3 18.7 %collective-permute-start.4 = (bf16[2,24,8192]{2,1,0:T(8,128)(2,1)S(1)}, bf16[2,24,8192]{2,1,0:T(8,128)(2,1)S(1)}, u32[]{:S(2)}, u32[]{:S(2)}) collective-permute-start(bf16[2,24,8192]{2,1,0:T(8,128)(2,1)S(1)} %collective-permute-done.3), channel_id=1, source_target_pairs={{0,1},{1,2},{2,3},{3,4},{4,5},{5,6},{6,7},{7,0},{8,9},{9,10},{10,1... | collective-permute-start | bytes 2359304 | tf_op jit(solution)/shard_map/ppermute | solution.py:27
  113.0 52.2 %copy-start.7 = (bf16[2,24,8192]{2,1,0:T(8,128)(2,1)}, bf16[2,24,8192]{2,1,0:T(8,128)(2,1)S(1)}, u32[]{:S(2)}) copy-start(bf16[2,24,8192]{2,1,0:T(8,128)(2,1)S(1)} %collective-permute-done.4) | copy-start | bytes 2359300
  113.0 17.8 %collective-permute-start.5 = (bf16[2,24,8192]{2,1,0:T(8,128)(2,1)S(1)}, bf16[2,24,8192]{2,1,0:T(8,128)(2,1)}, u32[]{:S(2)}, u32[]{:S(2)}) collective-permute-start(bf16[2,24,8192]{2,1,0:T(8,128)(2,1)S(1)} %collective-permute-done.4), channel_id=1, source_target_pairs={{0,1},{1,2},{2,3},{3,4},{4,5},{5,6},{6,7},{7,0},{8,9},{9,10},{10,1... | collective-permute-start | bytes 2359304 | tf_op jit(solution)/shard_map/ppermute | solution.py:27
  130.8 34.4 %collective-permute-start.6 = (bf16[2,24,8192]{2,1,0:T(8,128)(2,1)}, bf16[2,24,8192]{2,1,0:T(8,128)(2,1)}, u32[]{:S(2)}, u32[]{:S(2)}) collective-permute-start(bf16[2,24,8192]{2,1,0:T(8,128)(2,1)} %collective-permute-done.5), channel_id=1, source_target_pairs={{0,1},{1,2},{2,3},{3,4},{4,5},{5,6},{6,7},{7,0},{8,9},{9,10},{10,1... | collective-permute-start | bytes 2359304 | tf_op jit(solution)/shard_map/ppermute | solution.py:27
  165.2 11.4 %copy-start.2 = (bf16[2,24,8192]{2,1,0:T(8,128)(2,1)S(1)}, bf16[2,24,8192]{2,1,0:T(8,128)(2,1)}, u32[]{:S(2)}) copy-start(bf16[2,24,8192]{2,1,0:T(8,128)(2,1)} %param.8) | copy-start | bytes 2359300
  165.2 308.7 %all-reduce.8.cloned.1.call-start = ((), (), s32[]{:S(2)}) async-start(), calls=%async_computation.2 | async-start | bytes 6291456 | tf_op jit(solution)/shard_map/psum | solution.py:13
  165.2 8.5 %copy-start.4 = (bf16[2,24,8192]{2,1,0:T(8,128)(2,1)S(1)}, bf16[2,24,8192]{2,1,0:T(8,128)(2,1)}, u32[]{:S(2)}) copy-start(bf16[2,24,8192]{2,1,0:T(8,128)(2,1)} %copy-done.3) | copy-start | bytes 2359300
  408.9 310.8 %all-reduce.10.cloned.1.call-start = ((), (), s32[]{:S(2)}) async-start(), calls=%async_computation.3 | async-start | bytes 12582912 | tf_op jit(solution)/shard_map/psum | solution.py:44
  508.2 2.2 copy-start.5
  747.7 10.3 %copy-start.1 = (bf16[96,4096]{1,0:T(8,128)(2,1)S(1)}, bf16[96,4096]{1,0:T(8,128)(2,1)}, u32[]{:S(2)}) copy-start(bf16[96,4096]{1,0:T(8,128)(2,1)} %param.6) | copy-start | bytes 2359300
Sparse Core Ops, SparseCore 0:
  10.4 30.4 all-gather.1
  165.3 211.7 all-reduce.5
  409.1 64.7 all-reduce.7
  508.4 211.3 all-reduce.9
